TPU v7x, 32 devices: a whole 2x2x4 slice. The times are simulated.
32 devices in a mesh: seq: 8 (over z, y), blk: 4 (over x, core).
Axes of the slice: x: 2, y: 2, z: 4, core: 2. Of those that a mesh axis runs over, the one named last changes fastest.
Arguments:
- hidden_in: bfloat16 [16, 1024, 768], P('seq', 'blk'), may hold values from -6 to 6
- depth_group: int32 [16], P('seq'), may hold values from 0 to 2
- query_weight: bfloat16 [768, 768], replicated, may hold values from -0.21875 to 0.21875
- query_bias: bfloat16 [768], replicated, may hold values from -3 to 3
- key_weight: bfloat16 [768, 768], replicated, may hold values from -0.21875 to 0.21875
- value_weight: bfloat16 [768, 768], replicated, may hold values from -0.21875 to 0.21875
- value_bias: bfloat16 [768], replicated, may hold values from -0.119628906 to 0.119628906
- output_weight: bfloat16 [768, 768], replicated, may hold values from -4 to 4
- output_bias: bfloat16 [768], replicated, may hold values from -3 to 3
- attn_gain: bfloat16 [768], replicated, may hold values from 0.5 to 1.5
- attn_shift: bfloat16 [768], replicated, may hold values from -3 to 3
- inner_weight: bfloat16 [768, 3072], replicated, may hold values from -0.21875 to 0.21875
- inner_bias: bfloat16 [3072], replicated, may hold values from -3 to 3
- outer_weight: bfloat16 [3072, 768], replicated, may hold values from -0.109375 to 0.109375
- outer_bias: bfloat16 [768], replicated, may hold values from -3 to 3
- final_gain: bfloat16 [768], replicated, may hold values from 0.5 to 1.5
- final_shift: bfloat16 [768], replicated, may hold values from -3 to 3
- grad_out: bfloat16 [16, 1024, 768], P('seq', 'blk'), may hold values from -6 to 6
Outputs:
- hidden_out: bfloat16 [16, 1024, 768], P('seq', 'blk')
- grad_in: bfloat16 [16, 1024, 768], P('seq', 'blk')
- grad_query_weight: float32 [768, 768], P('seq')
- grad_query_bias: float32 [768], P('seq')
- grad_key_weight: float32 [768, 768], P('seq')
- grad_value_weight: float32 [768, 768], P('seq')
- grad_value_bias: float32 [768], P('seq')
- grad_output_weight: float32 [768, 768], P('seq')
- grad_output_bias: float32 [768], P('seq')
- grad_attn_gain: float32 [768], P('seq')
- grad_attn_shift: float32 [768], P('seq')
- grad_inner_weight: float32 [768, 3072], P('seq')
- grad_inner_bias: float32 [3072], P('seq')
- grad_outer_weight: float32 [3072, 768], P('seq')
- grad_outer_bias: float32 [768], P('seq')
- grad_final_gain: float32 [768], P('seq')
- grad_final_shift: float32 [768], P('seq')
All inputs are finite; a program needn't handle non-finite values.
Results may differ from a plain program's by a relative error of at most 0.02.
Values may be sent and summed in bfloat16 or wider, within the bound.
A program may use at most 128 MiB of HBM per device.

v0:
```python
import itertools
import math
from types import SimpleNamespace

import jax
import jax.numpy as jnp
from jax import lax
from jax.experimental import pallas as pl
from jax.experimental.pallas import tpu as pltpu
from jax.sharding import PartitionSpec as P

HD = 64
MESH = pl.DeviceIdType.MESH
BF = jnp.bfloat16
F32 = jnp.float32
LOG2E = math.log2(math.e)
SCALE2 = 0.125 * LOG2E
EPS = 1e-05

X, Y, Z0, Z1, C = range(5)
BITS = (Z1, Z0, Y)

PIECES = 12
OUTER, INNER, OUTPUT, PAIR = range(4)
S1, S2 = -1, -2
SMALL_ORDER = {S1: (C, Y, Z0, Z1, X), S2: (X, C, Y, Z0, Z1)}
FLOWS = (
    (OUTER, 0, 1, 0, 384, (Y, Z1, Z0, X)),
    (OUTER, 1, 1, 0, 384, (Z0, Y, X, Z1)),
    (OUTER, 2, 1, 0, 384, (Y, X, Z1, Z0)),
    (OUTER, 3, 1, 0, 384, (Z1, Y, Z0, X)),
    (INNER, 4, 1, 0, 384, (X, Y, Z0, Z1)),
    (INNER, 5, 1, 0, 384, (Z0, Y, X, Z1)),
    (INNER, 6, 1, 0, 384, (Y, Z0, X, Z1)),
    (INNER, 7, 1, 0, 384, (X, Y, Z1, Z0)),
    (OUTPUT, 11, 1, 0, 256, (X, Y, Z0, Z1)),
    (OUTPUT, 11, 1, 256, 128, (Z1, Y, Z0, X)),
    (PAIR, 8, 1, 0, 256, (X, Y, Z1, Z0)),
    (PAIR, 8, 1, 256, 128, (Y, Z0, X, Z1)),
    (PAIR + 1, 9, 1, 0, 256, (X, Z1, Y, Z0)),
    (PAIR + 1, 9, 1, 256, 128, (Y, Z1, Z0, X)),
    (PAIR + 2, 10, 1, 0, 128, (Y, Z0, Z1, X)),
    (PAIR + 2, 10, 1, 128, 128, (Z0, Y, Z1, X)),
    (PAIR + 2, 10, 1, 256, 128, (Y, Z0, Z1, X)),
)
PLAN = (
    (),
    ((0, -1), (1, -1)),
    ((2, -1), (3, -1)),
    (),
    ((4, -1), (5, -1)),
    ((6, -1),),
    ((7, -1),),
    (),
    ((0, 0),),
    ((S1, 0),),
    (),
    ((1, 0), (4, 0)),
    ((2, 0),),
    ((3, 0),),
    (),
    ((7, 0),),
    ((6, 0), (S1, 1)),
    ((0, 1),),
    ((8, 0), (1, 1), (5, 0)),
    ((2, 1), (9, 0)),
    ((4, 1), (6, 1)),
    ((S1, 2),),
    ((3, 1), (10, 0)),
    ((1, 2), (2, 2), (11, 0), (0, 2), (S1, 3), (6, 2)),
    ((4, 2), (7, 1)),
    ((1, 3), (3, 2), (8, 1)),
    ((12, 0), (6, 3), (2, 3), (0, 3)),
    ((S1, 4), (4, 3), (5, 1), (11, 1), (1, 4), (9, 1)),
    ((3, 3), (8, 2)),
    ((6, 4), (7, 2), (13, 0), (2, 4), (S2, 0)),
    (
        (0, 5), (1, 5), (3, 5), (4, 4), (6, 5), (2, 5), (S2, 1), (10, 1), (5, 2), (4, 5), (11, 2), (12, 1),
        (15, 0), (14, 0), (8, 3), (9, 2), (16, 0), (7, 3), (S2, 2), (13, 1), (12, 2), (14, 1), (15, 1), (10, 2),
        (5, 3), (16, 1), (S2, 3), (11, 3), (13, 2), (14, 2), (8, 4), (9, 3), (12, 3), (15, 2), (7, 4), (8, 5),
        (9, 5), (10, 3), (16, 2), (5, 4), (S2, 4), (11, 4), (7, 5), (13, 3), (14, 3), (5, 5), (12, 4), (11, 5),
        (15, 3), (13, 5), (14, 5), (10, 4), (12, 5), (16, 3), (15, 5), (10, 5), (16, 5),
    ),
)

QB, VB, OB, AG, AS, XB, FG, FS, IB = range(9)
HX, HC, HF, GO, GA, HO, GP, GI, AT = 0, 2, 3, 5, 6, 7, 8, 10, 11
EXCHANGES = 13


def nn(left, right):
    return jnp.dot(left, right, preferred_element_type=F32)


def nt(left, right):
    return lax.dot_general(left, right, (((1,), (1,)), ((), ())), preferred_element_type=F32)


def tn(left, right):
    return lax.dot_general(left, right, (((0,), (0,)), ((), ())), preferred_element_type=F32)


def fold8(values):
    rows, width = values.shape
    return jnp.sum(values.reshape(rows // 8, 8, width), axis=0)


def halves_rows(order, k):
    return X in order[: k + 1] and order.index(X) < 3


def recv_shape(flow, k, rows):
    part, f, nf, start, cols, order = flow
    free = [2 for ax in BITS if ax not in order[: k + 1]]
    return (nf, *free, rows // 2 if halves_rows(order, k) else rows, cols)


def layer_kernel(groups, names, *refs):
    r = SimpleNamespace(**dict(zip(names, refs)))
    seq = lax.axis_index("seq")
    blk = lax.axis_index("blk")
    x = lax.div(blk, 2)
    c = lax.rem(blk, 2)
    hi = lax.div(seq, groups)
    own = {X: x, Y: lax.rem(hi, 2), Z0: lax.rem(lax.div(hi, 2), 2), Z1: lax.div(hi, 4)}
    peers = {
        C: (seq, blk + 1 - 2 * c),
        X: (seq, blk + 2 - 4 * x),
        Y: (seq + (1 - 2 * own[Y]) * groups, blk),
        Z0: (seq + (1 - 2 * own[Z0]) * 2 * groups, blk),
        Z1: (seq + (1 - 2 * own[Z1]) * 4 * groups, blk),
    }
    tok, width = r.xall.shape[2:]
    slots = 4
    seq_len = slots * tok
    half = width // 2
    ff = r.wi.shape[1]
    pairs = half // 128
    me, at_x, at_c, at_xc = (x, c), (1 - x, c), (x, 1 - c), (1 - x, 1 - c)
    mine = (me, at_x)
    own_heads = pl.ds(pl.multiple_of(c * half, 128), half)
    other_heads = pl.ds(pl.multiple_of((1 - c) * half, 128), half)

    def seq_rows(slot, start=0, rows=tok):
        return pl.ds(pl.multiple_of((2 * slot[0] + slot[1]) * tok + start, rows), rows)

    def vec(i, start=0, size=width):
        return r.vec[:, pl.ds(width * i + start, size)]

    def pair_lanes(p, base=0):
        return pl.ds(pl.multiple_of(base * width + c * half + p * 128, 128), 128)

    def remote(src, dst, send, recv, peer):
        return pltpu.make_async_remote_copy(
            src_ref=src, dst_ref=dst, send_sem=send, recv_sem=recv, device_id=peers[peer], device_id_type=MESH
        )

    barrier = pltpu.get_barrier_semaphore()
    for peer in peers.values():
        pl.semaphore_signal(barrier, inc=1, device_id=peer, device_id_type=MESH)

    lcount = itertools.count()

    def fetch(src, dst):
        return pltpu.make_async_copy(src, dst, r.lsem.at[next(lcount)])

    first = [fetch(r.hid.at[x], r.xall.at[me])]
    for p in range(pairs):
        for i, w in enumerate((r.wq, r.wk, r.wv)):
            first.append(fetch(w.at[:, pair_lanes(p)], r.wcat.at[:, pl.ds((3 * p + i) * 128, 128)]))
    second = [
        fetch(r.go.at[x], r.gown.at[0]),
        fetch(r.wo_in, r.wo),
        fetch(r.wi_in, r.wi),
        fetch(r.wx_in, r.wx),
    ]
    for copy in first + second:
        copy.start()
    params = (r.qb, r.vb, r.ob, r.ag, r.sh, r.xb, r.fg, r.fs, r.ib)
    for i, ref in enumerate(params):
        r.vec[:, pl.ds(width * i, ref.shape[0])] = ref[...].astype(F32).reshape(1, ref.shape[0])
    r.sg8[...] = jnp.zeros_like(r.sg8)
    kept = jnp.where(r.dg[x] == 2, 0.0, 1.0).astype(F32)
    pl.semaphore_wait(barrier, len(peers))

    hrows = tok // 2

    def ex(i):
        if i == HC:
            src, dst, peer = r.hid.at[x], r.xall.at[me], C
        elif i == GO:
            src, dst, peer = r.go.at[1 - x], r.gown.at[1], X
        elif i == GA:
            src = dst = r.ga.at[:, c]
            peer = C
        elif i == HO:
            src, dst, peer = r.ga.at[at_x], r.hout.at[x], X
        elif i == GI:
            src, dst, peer = r.inn.at[pl.ds(tok, tok)], r.gin.at[x], X
        else:
            src, dst, peer = r.gffn.at[pl.ds((i - GP) * tok, tok)], r.xall.at[(at_c, at_xc)[i - GP]], C
        return remote(src, dst, r.ex_s.at[i], r.ex_r.at[i], peer)

    def ex_in(i):
        hs = pl.ds(i * hrows, hrows)
        return remote(r.hid.at[1 - x, hs], r.xall.at[x, c, hs], r.ex_s.at[HX + i], r.ex_r.at[HX + i], X)

    def ex_on(i):
        ref = r.xall.at[1 - x, c, pl.ds(i * hrows, hrows)]
        return remote(ref, ref, r.ex_s.at[HF + i], r.ex_r.at[HF + i], C)

    def ex_att(i):
        ref = r.att.at[:, 1 - c + i * (2 * c - 1), :, own_heads]
        return remote(ref, ref, r.ex_s.at[AT + i], r.ex_r.at[AT + i], C)

    ex_in(0).start()
    ex_in(1).start()
    ex(HC).start()
    ex(GO).start()

    lane_head = lax.broadcasted_iota(jnp.int32, (tok, 128), 1) // HD
    ones = jnp.ones((seq_len, 128), BF)
    for p in range(pairs):
        r.vp[p, :, pl.ds(128, 128)] = ones

    def project(slot, start, rows):
        out = nn(r.xall[(*slot, pl.ds(start, rows), slice(None))], r.wcat[...])
        at = seq_rows(slot, start, rows)
        for p in range(pairs):
            lanes = pl.ds(p * 128, 128)
            base = 3 * p * 128
            r.q[at, lanes] = (out[:, base : base + 128] + r.vec[:, pair_lanes(p, QB)]).astype(BF)
            key = out[:, base + 128 : base + 256].astype(BF)
            r.k[at, lanes] = key
            r.kt[lanes, at] = key.T
            r.vp[p, at, pl.ds(0, 128)] = (out[:, base + 256 : base + 384] + r.vec[:, pair_lanes(p, VB)]).astype(BF)

    for copy in first:
        copy.wait()
    ex(HC).wait_recv()

    @pl.loop(0, 2)
    def _(i):
        project((x, i), 0, tok)

    @pl.loop(0, 2)
    def _(i):
        ex_in(i).wait_recv()
        ex_on(i).start()
        project(at_x, i * hrows, hrows)

    @pl.loop(0, 2)
    def _(i):
        ex_on(i).wait_recv()
        project(at_xc, i * hrows, hrows)

    def forward(p, slot):
        lanes = pl.ds(p * 128, 128)
        rows = seq_rows(slot)
        qp = r.q[rows, lanes]
        outs, sums = [], []
        for h in range(2):
            qm = jnp.where(lane_head == h, qp, jnp.zeros_like(qp))
            s = nn(qm, r.kt[lanes, :])
            top = jnp.max(s, axis=1, keepdims=True)
            pt = jnp.exp2((s - top) * SCALE2).astype(BF)
            o = nn(pt, r.vp[p])
            sums.append(top * SCALE2 + jnp.log2(o[:, 128:]))
            outs.append(o[:, :128] / o[:, 128:])
        r.att[(*slot, slice(None), pair_lanes(p))] = jnp.where(lane_head == 0, outs[0], outs[1]).astype(BF)
        both = jnp.where(lane_head == 0, sums[0], sums[1]).T
        for h in range(2):
            r.lse[2 * p + h, :, rows] = both[h * HD : h * HD + 1]

    @pl.loop(0, 2)
    def _(i):
        core = 1 - c + i * (2 * c - 1)
        for p in range(pairs):
            forward(p, (x, core))
            forward(p, (1 - x, core))
        ex_att(i).start()

    for copy in second:
        copy.wait()
    chunk = tok // 2

    def own_rows(i):
        inner = pl.ds((i % 2) * chunk, chunk)
        return mine[i // 2], i // 2, inner, pl.ds(i * chunk, chunk)

    def fold_in(i, values):
        at = pl.ds(width * i, values.shape[1])
        r.sg8[:, at] += fold8(values)

    def heads_out(i, heads):
        return nn(r.att[(*mine[i], slice(None), heads)], r.wo[heads, :])

    for i in range(2):
        r.acc[pl.ds(i * tok, tok), :] = heads_out(i, own_heads)
    ex_att(0).wait_recv()
    for i in range(2):
        r.acc[pl.ds(i * tok, tok), :] += heads_out(i, other_heads)

    for i in range(4):
        slot, which, inner, rows = own_rows(i)
        v = r.acc[rows, :] + vec(OB) + r.xall[(*slot, inner, slice(None))].astype(F32)
        cen = v - jnp.mean(v, axis=-1, keepdims=True)
        rstd = lax.rsqrt(jnp.mean(cen * cen, axis=-1, keepdims=True) + EPS)
        xh = cen * rstd
        normed = xh * vec(AG) + vec(AS)
        r.xh[rows, :] = xh
        r.dva[rows, pl.ds(0, 1)] = rstd
        r.acc[rows, :] = normed
        r.inn[rows, :] = normed.astype(BF)

    tile = 512

    def activate(j):
        start = pl.multiple_of(j * tile, tile)
        at = pl.ds(start, tile)
        pre = nn(r.inn[...], r.wi[:, at]) + r.vec[:, pl.ds(pl.multiple_of(width * IB + start, 128), tile)]
        phi = 0.5 + 0.5 * lax.erf(pre * math.sqrt(0.5))
        dens = jnp.exp2(pre * pre * (-0.5 * LOG2E)) * (1.0 / math.sqrt(2.0 * math.pi))
        r.act[:, at] = (pre * phi).astype(BF)
        r.gp[:, at] = (phi + pre * dens).astype(BF)

    @pl.loop(0, 2)
    def _(i):
        for j in range(ff // tile // 2):
            activate(i * (ff // tile // 2) + j)

    for j in range(width // 256):
        at = pl.ds(j * 256, 256)
        r.acc[:, at] += nn(r.act[...], r.wx[:, at])

    ex(GO).wait_recv()
    for i in range(4):
        slot, which, inner, rows = own_rows(i)
        xf = r.xall[(*slot, inner, slice(None))].astype(F32)
        v = r.acc[rows, :] + vec(XB)
        cen = v - jnp.mean(v, axis=-1, keepdims=True)
        rstd = lax.rsqrt(jnp.mean(cen * cen, axis=-1, keepdims=True) + EPS)
        xh = cen * rstd
        out = kept * (xh * vec(FG) + vec(FS)) + (1.0 - kept) * xf
        r.ga[(*slot, inner, slice(None))] = out.astype(BF)
        g = kept * r.gown[which, inner, :].astype(F32)
        fold_in(FG, g * xh)
        fold_in(FS, g)
        gx = g * vec(FG)
        m1 = jnp.mean(gx, axis=-1, keepdims=True)
        m2 = jnp.mean(gx * xh, axis=-1, keepdims=True)
        gs = rstd * (gx - m1 - xh * m2)
        low = gs.astype(BF)
        r.acc[rows, :] = gs
        r.gffn[rows, :] = low
        fold_in(XB, low.astype(F32))

    ex(HO).start()
    hout_local = fetch(r.ga.at[me], r.hout.at[x])
    hout_local.start()

    rows_f, cols_f = r.dc.shape[-2:]
    x_rows = pl.ds(pl.multiple_of(x * (rows_f // 2), 16), rows_f // 2)

    def pieces(flow):
        f, nf = flow[1:3]
        return r.d2.at[c, pl.ds(f, nf)] if f < 8 else r.dc.at[pl.ds(f - 8, nf)]

    def view(flow, k, send):
        part, f, nf, start, cols, order = flow
        idx = [slice(None)] * 3
        row = pl.ds(0, rows_f)
        for j, ax in enumerate(order[: k + 1]):
            want = 1 - own[ax] if (j == k and send) else own[ax]
            if ax != X:
                idx[BITS.index(ax)] = want
            elif j < 3:
                row = pl.ds(pl.multiple_of(want * (rows_f // 2), 16), rows_f // 2)
        return (slice(None), *idx, row, pl.ds(start, cols))

    def hop(i, k):
        flow = FLOWS[i]
        src = pieces(flow).at[view(flow, k, True)]
        return remote(src, r.land[i][k], r.rs_s.at[i, k], r.rs_r.at[i, k], flow[5][k])

    def add_in(i, k):
        flow = FLOWS[i]
        nf, order = flow[2], flow[5]
        idx = list(view(flow, k, False))
        ref = pieces(flow)
        free = [ax for ax in BITS if ax not in order[: k + 1]]
        for n in range(nf):
            idx[0] = n
            for combo in itertools.product((0, 1), repeat=len(free)):
                for ax, bit in zip(free, combo):
                    idx[1 + BITS.index(ax)] = bit
                at = tuple(idx)
                ref[at] = ref[at] + r.land[i][k][(n, *combo, slice(None), slice(None))]

    def spread(i, k):
        part, f, nf, start, cols, order = FLOWS[i]
        rows = x_rows if k == 4 else pl.ds(0, rows_f)
        ref = r.fin.at[pl.ds(f, nf), c, rows, pl.ds(start, cols)]
        return remote(ref, ref, r.rs_s.at[i, k], r.rs_r.at[i, k], X if k == 4 else C)

    def core_sum(i):
        part, f, nf, start, cols, order = FLOWS[i]
        at = pl.ds(f, nf)
        return remote(r.d2.at[1 - c, at], r.rc.at[at], r.rs_s.at[i, 6], r.rs_r.at[i, 6], C)

    def small(which, k):
        send, recv = (r.s1s, r.s1r) if which == S1 else (r.s2s, r.s2r)
        at = k if which == S1 else 5 + k
        return remote(send.at[k], recv.at[k], r.sm_s.at[at], r.sm_r.at[at], SMALL_ORDER[which][k])

    def step(i, k):
        if i < 0:
            send, recv = (r.s1s, r.s1r) if i == S1 else (r.s2s, r.s2r)
            small(i, k).wait_recv()
            send[k + 1] = send[k] + recv[k]
            if k < 4:
                small(i, k + 1).start()
            return
        flow = FLOWS[i]
        part, f, nf, start, cols, order = flow
        if k == -1:
            core_sum(i).wait_recv()
            ref = pieces(flow)
            for combo in itertools.product(range(nf), (0, 1), (0, 1), (0, 1)):
                ref[combo] = ref[combo] + r.rc[(f + combo[0], *combo[1:])]
            hop(i, 0).start()
        elif k < 3:
            hop(i, k).wait_recv()
            add_in(i, k)
            hop(i, k + 1).start()
        elif k == 3:
            hop(i, 3).wait_recv()
            rows = pl.ds(0, rows_f) if order[3] == X else x_rows
            at = pl.ds(start, cols)
            for n in range(nf):
                mine_part = pieces(flow)[(n, own[Z1], own[Z0], own[Y], rows, at)]
                r.fin[f + n, c, rows, at] = mine_part + r.land[i][3][n]
            spread(i, 5 if order[3] == X else 4).start()
        elif k == 4:
            spread(i, 4).wait_recv()
            spread(i, 5).start()
        else:
            spread(i, 5).wait_recv()

    plan = iter(PLAN)

    def tick():
        for i, k in next(plan):
            step(i, k)

    def begin(part):
        for i, flow in enumerate(FLOWS):
            if flow[0] == part:
                (core_sum(i) if flow[1] < 8 else hop(i, 0)).start()

    outer_rows = ff // 8

    @pl.loop(0, 2)
    def _(i):
        for j in range(4):
            at = pl.ds(pl.multiple_of((4 * i + j) * outer_rows, 128), outer_rows)
            val = tn(r.act[:, at], r.gffn[...]).astype(BF)
            for f in range(4):
                for h in range(2):
                    part = val[f * rows_f : (f + 1) * rows_f, h * cols_f : (h + 1) * cols_f]
                    r.d2[h, f, i, j // 2, j % 2] = part

    begin(OUTER)
    tick()

    tile = ff // 4

    @pl.loop(0, 2)
    def _(i):
        for j in range(2):
            start = pl.multiple_of((2 * i + j) * tile, tile)
            at = pl.ds(start, tile)
            gpre = (nt(r.gffn[...], r.wx[at, :]) * r.gp[:, at].astype(F32)).astype(BF)
            r.gp[:, at] = gpre
            r.sg8[:, pl.ds(pl.multiple_of(width * IB + start, 128), tile)] = fold8(gpre.astype(F32))

    tick()

    @pl.loop(0, 2)
    def _(i):
        for h in range(2):
            at = pl.ds(pl.multiple_of((2 * h + i) * tile, tile), tile)
            val = tn(r.inn[...], r.gp[:, at]).astype(BF)
            for m in range(2):
                part = val[:, m * cols_f : (m + 1) * cols_f]
                r.d2[h, 4 + 2 * i + m] = part.reshape(2, 2, 2, rows_f, cols_f)
        for n in range(2):

            @pl.when(i == n)
            def _():
                for g, flow in enumerate(FLOWS):
                    if flow[0] == INNER and (flow[1] + flow[2] - 1) // 2 == 2 + n:
                        core_sum(g).start()
                tick()

    for j in range(3):
        at = pl.ds(j * 256, 256)
        r.acc[:, at] += nt(r.gp[...], r.wi[at, :])
        tick()

    ex(HO).wait_send()
    hout_local.wait()
    for i in range(4):
        slot, which, inner, rows = own_rows(i)
        g = r.acc[rows, :]
        xh = r.xh[rows, :]
        fold_in(AG, g * xh)
        fold_in(AS, g)
        gx = g * vec(AG)
        m1 = jnp.mean(gx, axis=-1, keepdims=True)
        m2 = jnp.mean(gx * xh, axis=-1, keepdims=True)
        gs = r.dva[rows, pl.ds(0, 1)] * (gx - m1 - xh * m2)
        low = gs.astype(BF)
        r.acc[rows, :] = gs
        r.ga[(*slot, inner, slice(None))] = low
        fold_in(OB, low.astype(F32))

    xt = r.wi.at[:, pl.ds(0, seq_len)]
    xt[...] = r.xall[...].reshape(seq_len, width).T
    for i in range(2):
        ex_on(i).wait_send()
    ex(GA).start()
    late = 2 * width
    r.s1s[0] = jnp.sum(r.sg8[:, pl.ds(late, r.s1s.shape[2])], axis=0, keepdims=True)
    small(S1, 0).start()
    tick()

    def dqkv(p):
        rows = pl.ds(pl.multiple_of(lax.div(p, 2) * seq_len, 1024), seq_len)
        return r.wx.at[rows, pl.ds(pl.multiple_of(lax.rem(p, 2) * 384, 128), 384)]

    do = r.wx.at[pl.ds(seq_len, seq_len), pl.ds(384, half)]

    def upstream(slot):
        do[seq_rows(slot), :] = nt(r.ga[slot], r.wo[own_heads, :]).astype(BF)

    upstream(me)
    upstream(at_x)
    tick()
    ex(GA).wait_recv()
    upstream(at_c)
    upstream(at_xc)

    for p in range(pairs):
        at = r.att[:, :, :, pair_lanes(p)].reshape(seq_len, 128)
        prod = (at.astype(F32) * do[:, pl.ds(p * 128, 128)].astype(F32)).T
        for h in range(2):
            r.delta[2 * p + h] = jnp.sum(prod[h * HD : (h + 1) * HD], axis=0, keepdims=True)
    tick()

    ex_att(1).wait_recv()
    att_all = r.att[...].reshape(seq_len, width)
    ga_cols = r.ga[:, :, :, own_heads].reshape(seq_len, half)
    r.dc[3] = tn(att_all, ga_cols).astype(BF).reshape(2, 2, 2, rows_f, cols_f)
    begin(OUTPUT)
    tick()

    r.xh[...] = jnp.zeros_like(r.xh)
    steps = [[next(plan) for _ in range(slots + 2)] for _ in range(pairs)]

    def tick_at(p, j):
        for n in range(pairs):
            if steps[n][j]:

                @pl.when(p == n)
                def _():
                    for i, k in steps[n][j]:
                        step(i, k)

    @pl.loop(0, pairs)
    def _(p):
        lanes = pl.ds(pl.multiple_of(p * 128, 128), 128)
        for t in range(slots):
            rows = pl.ds(t * tok, tok)
            qp = r.q[rows, lanes]
            dp = do[rows, lanes]
            kp = r.k[:, lanes]
            vp = r.vp[p, :, pl.ds(0, 128)]
            zero = jnp.zeros_like(qp)
            dqs = []
            for h in range(2):
                qm = jnp.where(lane_head == h, qp, zero)
                dm = jnp.where(lane_head == h, dp, zero)
                pt = jnp.exp2(nt(kp, qm) * SCALE2 - r.lse[2 * p + h, :, rows])
                ds = (pt * (nt(vp, dm) - r.delta[2 * p + h, :, rows])).astype(BF)
                dv, dk = nn(pt.astype(BF), dm), nn(ds, qm)
                if t == 0 and h == 0:
                    r.dva[...] = dv
                    r.dka[...] = dk
                else:
                    r.dva[...] += dv
                    r.dka[...] += dk
                dqs.append(nn(r.kt[pl.ds(pl.multiple_of(p * 128 + h * HD, HD), HD), :], ds))
            both = (jnp.concatenate(dqs, axis=0) * 0.125).astype(BF)
            dqkv(p)[rows, pl.ds(0, 128)] = both.T
            if t == slots - 1:
                dqkv(p)[:, pl.ds(128, 128)] = (r.dka[...] * 0.125).astype(BF)
                dqkv(p)[:, pl.ds(256, 128)] = r.dva[...].astype(BF)
            tick_at(p, t)

        weights = r.wcat[:, pl.ds(pl.multiple_of(p * 384, 128), 384)]

        def partial(slot):
            return nt(dqkv(p)[seq_rows(slot), :], weights)

        for i in (1, 0):
            r.xh[pl.ds(i * tok, tok), :] += partial((at_c, at_xc)[i])

        @pl.when(p == pairs - 1)
        def _():
            for i in (1, 0):
                rows = pl.ds(i * tok, tok)
                r.gffn[rows, :] = r.xh[rows, :].astype(BF)
                ex(GP + i).start()

        r.dc[p] = nn(xt[...], dqkv(p)[...]).astype(BF).reshape(2, 2, 2, rows_f, cols_f)
        r.sg8[:, pair_lanes(p, QB)] = fold8(dqkv(p)[:, pl.ds(0, 128)].astype(F32))
        r.sg8[:, pair_lanes(p, VB)] = fold8(dqkv(p)[:, pl.ds(256, 128)].astype(F32))
        for n in range(pairs):

            @pl.when(p == n)
            def _():
                begin(PAIR + n)
                if n == pairs - 1:
                    r.s2s[0] = jnp.sum(r.sg8[:, pl.ds(0, late)], axis=0, keepdims=True)
                    small(S2, 0).start()

        tick_at(p, slots)
        for i in (1, 0):
            r.acc[pl.ds(i * tok, tok), :] += partial(mine[i])
        tick_at(p, slots + 1)

    for i in (1, 0):
        rows = pl.ds(i * tok, tok)
        ex(GP + i).wait_recv()
        total = r.acc[rows, :] + r.xall[mine[i]].astype(F32) + (1.0 - kept) * r.gown[i].astype(F32)
        r.inn[rows, :] = total.astype(BF)
        if i == 1:
            ex(GI).start()
    gin_local = fetch(r.inn.at[pl.ds(0, tok)], r.gin.at[x])
    gin_local.start()
    tick()
    tick()
    r.sout[:, pl.ds(0, late)] = r.s2s[5]
    r.sout[:, pl.ds(late, r.s1s.shape[2])] = r.s1s[5]

    ex(HO).wait_recv()
    ex(GI).wait_recv()
    gin_local.wait()
    for i in (HC, GO, GA, GP, GP + 1, GI):
        ex(i).wait_send()
    for i in range(2):
        ex_in(i).wait_send()
        ex_att(i).wait_send()
    for k in range(5):
        small(S1, k).wait_send()
        small(S2, k).wait_send()
    for i, flow in enumerate(FLOWS):
        for k in range(4):
            hop(i, k).wait_send()
        if flow[5][3] != X:
            spread(i, 4).wait_send()
        spread(i, 5).wait_send()
        if flow[1] < 8:
            core_sum(i).wait_send()


def finish_kernel(n_seq, names, *refs):
    r = SimpleNamespace(**dict(zip(names, refs)))
    pairs = ((r.hout_in, r.hout), (r.gin_in, r.gin))
    arrive = [pltpu.make_async_copy(pair[0], r.through.at[i], r.sem.at[i]) for i, pair in enumerate(pairs)]
    leave = [pltpu.make_async_copy(r.through.at[i], pair[1], r.sem.at[2 + i]) for i, pair in enumerate(pairs)]
    for copy in arrive:
        copy.start()
    for before, after in zip(arrive, leave):
        before.wait()
        after.start()
    rows_f, cols_f = r.fin.shape[2:]
    half = cols_f
    outs = (r.outer, r.inner, r.output, r.query, r.key, r.value)
    made = (r.t_outer, r.t_inner, r.t_output, r.t_query, r.t_key, r.t_value)
    done = [pltpu.make_async_copy(src, dst, r.sem.at[4 + i]) for i, (src, dst) in enumerate(zip(made, outs))]

    def take(f):
        return pltpu.make_async_copy(r.fin.at[f], r.got.at[f], r.sem.at[10 + f])

    for f in range(PIECES):
        take(f).start()
    for f in range(4):
        take(f).wait()
        for h in range(2):
            r.t_outer[pl.ds(f * rows_f, rows_f), pl.ds(h * half, half)] = r.got[f, h].astype(F32)
    done[0].start()
    for f in range(4):
        take(4 + f).wait()
        for h in range(2):
            r.t_inner[:, pl.ds((4 * h + f) * cols_f, cols_f)] = r.got[4 + f, h].astype(F32)
    done[1].start()
    for f in range(8, PIECES):
        take(f).wait()
    for h in range(2):
        r.t_output[:, pl.ds(h * half, half)] = r.got[11, h].astype(F32)
    done[2].start()
    for i, ref in enumerate(made[3:]):
        for h in range(2):
            for p in range(half // 128):
                part = r.got[8 + p, h, :, pl.ds(i * 128, 128)].astype(F32)
                ref[:, pl.ds(h * half + p * 128, 128)] = part
        done[3 + i].start()
    seq = lax.axis_index("seq")
    width = 2 * half
    share = width // n_seq
    for i in range(8):
        r.rows[pl.ds(i, 1), :] = r.sout[:, pl.ds(i * width, width)]
    turned = pltpu.roll(r.rows[...], lax.rem(width - seq * share, width), 1)
    for i, ref in enumerate((r.qb, r.vb, r.ob, r.ag, r.sh, r.xb, r.fg, r.fs)):
        ref[...] = turned[i, :share]
    ib = r.ib.shape[0]
    full = r.sout.shape[1] - 8 * width
    r.wide[...] = jnp.broadcast_to(r.sout[:, pl.ds(8 * width, full)], (8, full))
    r.ib[...] = pltpu.roll(r.wide[...], lax.rem(full - seq * ib, full), 1)[0, :ib]
    for copy in leave + done:
        copy.wait()


def call(kernel, ins, outs, scratch, params, name, land=()):
    names = [*ins, *outs, *scratch]

    def body(*refs):
        extra = refs[len(names) :]
        shelf = iter(extra)
        nested = [[next(shelf) for _ in group] for group in land]
        kernel([*names, *(("land",) if land else ())], *refs[: len(names)], *((nested,) if land else ()))

    res = pl.pallas_call(
        body,
        out_shape=[jax.ShapeDtypeStruct(e[0], e[1]) for e in outs.values()],
        in_specs=[e[1] for e in ins.values()],
        out_specs=[e[2] for e in outs.values()],
        scratch_shapes=[*scratch.values(), *(e for group in land for e in group)],
        compiler_params=params,
        name=name,
    )(*[e[0] for e in ins.values()])
    return SimpleNamespace(**dict(zip(outs, res)))


def build(mesh):
    n_seq = mesh.shape["seq"]
    groups = n_seq // 8

    def local(
        hidden_in,
        depth_group,
        query_weight,
        query_bias,
        key_weight,
        value_weight,
        value_bias,
        output_weight,
        output_bias,
        attn_gain,
        attn_shift,
        inner_weight,
        inner_bias,
        outer_weight,
        outer_bias,
        final_gain,
        final_shift,
        grad_out,
    ):
        seqs, tok, width = hidden_in.shape
        ff = inner_weight.shape[1]
        seq_len = 4 * tok
        half = width // 2
        heads = half // HD
        pairs = half // 128
        rows_f, cols_f = width // 8, half
        small, late = 8 * width + ff, 2 * width
        hbm = pl.BlockSpec(memory_space=pl.ANY)
        vmem = pl.BlockSpec(memory_space=pltpu.VMEM)
        v = pltpu.VMEM
        dma = pltpu.SemaphoreType.DMA
        o = call(
            lambda *refs: layer_kernel(groups, *refs),
            dict(
                qb=(query_bias, vmem),
                vb=(value_bias, vmem),
                ob=(output_bias, vmem),
                ag=(attn_gain, vmem),
                sh=(attn_shift, vmem),
                xb=(outer_bias, vmem),
                fg=(final_gain, vmem),
                fs=(final_shift, vmem),
                ib=(inner_bias, vmem),
                dg=(depth_group, pl.BlockSpec(memory_space=pltpu.SMEM)),
                hid=(hidden_in, hbm),
                go=(grad_out, hbm),
                wq=(query_weight, hbm),
                wk=(key_weight, hbm),
                wv=(value_weight, hbm),
                wo_in=(output_weight, hbm),
                wi_in=(inner_weight, hbm),
                wx_in=(outer_weight, hbm),
            ),
            dict(
                hout=((seqs, tok, width), BF, hbm),
                gin=((seqs, tok, width), BF, hbm),
                fin=((PIECES, 2, rows_f, cols_f), BF, vmem),
                sout=((1, small), F32, vmem),
            ),
            dict(
                vec=v((1, small), F32),
                xall=v((2, 2, tok, width), BF),
                gown=v((2, tok, width), BF),
                wcat=v((width, 3 * half), BF),
                wo=v((width, width), BF),
                wi=v((width, ff), BF),
                wx=v((ff, width), BF),
                q=v((seq_len, half), BF),
                k=v((seq_len, half), BF),
                kt=v((half, seq_len), BF),
                vp=v((pairs, seq_len, 256), BF),
                lse=v((heads, 1, seq_len), F32),
                delta=v((heads, 1, seq_len), F32),
                att=v((2, 2, tok, width), BF),
                ga=v((2, 2, tok, width), BF),
                act=v((2 * tok, ff), BF),
                gp=v((2 * tok, ff), BF),
                inn=v((2 * tok, width), BF),
                gffn=v((2 * tok, width), BF),
                xh=v((2 * tok, width), F32),
                acc=v((2 * tok, width), F32),
                dka=v((seq_len, 128), F32),
                dva=v((seq_len, 128), F32),
                d2=v((2, 8, 2, 2, 2, rows_f, cols_f), BF),
                rc=v((8, 2, 2, 2, rows_f, cols_f), BF),
                dc=v((4, 2, 2, 2, rows_f, cols_f), BF),
                sg8=v((8, small), F32),
                s1s=v((6, 1, small - late), F32),
                s1r=v((5, 1, small - late), F32),
                s2s=v((6, 1, late), F32),
                s2r=v((5, 1, late), F32),
                lsem=dma((7 + 3 * pairs,)),
                ex_s=dma((EXCHANGES,)),
                ex_r=dma((EXCHANGES,)),
                rs_s=dma((len(FLOWS), 7)),
                rs_r=dma((len(FLOWS), 7)),
                sm_s=dma((10,)),
                sm_r=dma((10,)),
            ),
            pltpu.CompilerParams(collective_id=0, has_side_effects=True, vmem_limit_bytes=64 * 1024 * 1024),
            "layer",
            [[v(recv_shape(flow, k, rows_f), BF) for k in range(4)] for flow in FLOWS],
        )

        rows = [[g * groups + i for i in range(groups)] for g in range(8)]
        sout = o.sout
        if groups > 1:
            sout = lax.psum(sout, "seq", axis_index_groups=rows)
        mat, one = ((rows_f, width), F32, hbm), ((width // n_seq,), F32, vmem)
        staged = v((rows_f, width), F32)
        f = call(
            lambda *refs: finish_kernel(n_seq, *refs),
            dict(hout_in=(o.hout, hbm), gin_in=(o.gin, hbm), fin=(o.fin, hbm), sout=(sout, vmem)),
            dict(
                hout=(o.hout.shape, BF, hbm),
                gin=(o.gin.shape, BF, hbm),
                query=mat,
                key=mat,
                value=mat,
                output=mat,
                inner=((rows_f, ff), F32, hbm),
                outer=((ff // 8, width), F32, hbm),
                qb=one,
                vb=one,
                ob=one,
                ag=one,
                sh=one,
                xb=one,
                fg=one,
                fs=one,
                ib=((ff // n_seq,), F32, vmem),
            ),
            dict(
                sem=dma((10 + PIECES,)),
                got=v((PIECES, 2, rows_f, cols_f), BF),
                t_query=staged,
                t_key=staged,
                t_value=staged,
                t_output=staged,
                t_inner=v((rows_f, ff), F32),
                t_outer=v((ff // 8, width), F32),
                through=v((2, seqs, tok, width), BF),
                rows=v((8, width), F32),
                wide=v((8, ff), F32),
            ),
            pltpu.CompilerParams(vmem_limit_bytes=64 * 1024 * 1024),
            "finish",
        )

        def across(values):
            if groups == 1:
                return values
            return lax.psum_scatter(values, "seq", scatter_dimension=0, axis_index_groups=rows, tiled=True)

        return (
            f.hout,
            f.gin,
            across(f.query),
            f.qb,
            across(f.key),
            across(f.value),
            f.vb,
            across(f.output),
            f.ob,
            f.ag,
            f.sh,
            across(f.inner),
            f.ib,
            across(f.outer),
            f.xb,
            f.fg,
            f.fs,
        )

    return local


def solution(mesh):
    rows = P("seq", "blk", None)
    placed = (rows, P("seq"), *([P()] * 15), rows)
    mat, one = P("seq", None), P("seq")
    return jax.shard_map(
        build(mesh),
        mesh=mesh,
        in_specs=placed,
        out_specs=(rows, rows, mat, one, mat, mat, one, mat, one, one, one, mat, one, mat, one, one, one),
        check_vma=False,
    )
```

profile of v0, /device:TPU:1, one launch (start us, length us, event | category | flops | bytes accessed | tf_op | source)
XLA Modules:
  0.0 120.0 jit_solution(13949250211230947848)
XLA Ops:
  0.7 112.9 %layer.1 = (bf16[2,256,768]{2,1,0:T(8,128)(2,1)}, bf16[2,256,768]{2,1,0:T(8,128)(2,1)}, bf16[12,2,96,384]{3,2,1,0:T(8,128)(2,1)}, f32[1,9216]{1,0:T(1,128)}) custom-call(bf16[768]{0:T(1024)(128)(2,1)} %refs_0_.1, bf16[768]{0:T(1024)(128)(2,1)} %refs_1_.1, bf16[768]{0:T(1024)(128)(2,1)} %refs_2_.1, bf16[768]{0:T(1024)(128)(2,1)} %refs_3_.1, ...), custom_call_target="tpu_custom_call" | custom-call | tf_op jit(solution)/shard_map/layer/pallas_call | solution.py:745
  113.6 6.2 %finish.1 = (bf16[2,256,768]{2,1,0:T(8,128)(2,1)}, bf16[2,256,768]{2,1,0:T(8,128)(2,1)}, f32[96,768]{1,0:T(8,128)}, f32[96,768]{1,0:T(8,128)}, f32[96,768]{1,0:T...) custom-call(bf16[2,256,768]{2,1,0:T(8,128)(2,1)} %get-tuple-element., ...), custom_call_target="tpu_custom_call" | custom-call | tf_op jit(solution)/shard_map/finish/pallas_call | solution.py:745
where the time goes:
time: 120 us
  Pallas kernels  119 us (99%)
    pallas_call x2, Pallas kernels, call(): pl.pallas_call(body, out_shape=[jax.ShapeDtypeStruct(e[0], e[1]) for e in...  119 us

commit v1 on v0

v1 whole, which is shorter than its diff:
```python
import itertools
import math
from types import SimpleNamespace

import jax
import jax.numpy as jnp
from jax import lax
from jax.experimental import pallas as pl
from jax.experimental.pallas import tpu as pltpu
from jax.sharding import PartitionSpec as P

HD = 64
MESH = pl.DeviceIdType.MESH
BF = jnp.bfloat16
F32 = jnp.float32
LOG2E = math.log2(math.e)
SCALE2 = 0.125 * LOG2E
EPS = 1e-05

X, Y, Z0, Z1, C = range(5)
BITS = (Z1, Z0, Y)

PIECES = 12
OUTER, INNER, OUTPUT, PAIR = range(4)
S1, S2 = -1, -2
SMALL_ORDER = {S1: (C, Y, Z0, Z1, X), S2: (X, C, Y, Z0, Z1)}
FLOWS = (
    (OUTER, 0, 1, 0, 384, (Z0, X, Z1, Y)),
    (OUTER, 1, 1, 0, 384, (Y, Z1, Z0, X)),
    (OUTER, 2, 1, 0, 384, (X, Y, Z0, Z1)),
    (OUTER, 3, 1, 0, 384, (Z0, Y, Z1, X)),
    (INNER, 4, 1, 0, 384, (Y, Z1, Z0, X)),
    (INNER, 5, 1, 0, 384, (Y, X, Z0, Z1)),
    (INNER, 6, 1, 0, 384, (X, Y, Z0, Z1)),
    (INNER, 7, 1, 0, 384, (Z0, Y, Z1, X)),
    (OUTPUT, 11, 1, 0, 384, (X, Z0, Y, Z1)),
    (PAIR, 8, 1, 0, 384, (X, Y, Z0, Z1)),
    (PAIR + 1, 9, 1, 0, 384, (Y, Z0, Z1, X)),
    (PAIR + 2, 10, 1, 0, 128, (Z0, Y, Z1, X)),
    (PAIR + 2, 10, 1, 128, 128, (X, Z1, Y, Z0)),
    (PAIR + 2, 10, 1, 256, 128, (Y, Z0, Z1, X)),
)
PLAN = (
    (),
    ((0, -1), (1, -1)),
    ((2, -1), (3, -1)),
    (),
    (),
    ((S1, 0), (4, -1), (0, 0), (1, 0)),
    ((5, -1),),
    ((6, -1), (S1, 1), (7, -1)),
    (),
    ((2, 0),),
    ((0, 1), (1, 1), (4, 0), (3, 0), (S1, 2)),
    (),
    ((6, 0), (5, 0), (0, 2)),
    ((2, 1), (7, 0)),
    ((8, 0), (3, 1), (1, 2), (4, 1)),
    ((S1, 3), (6, 1), (2, 2), (0, 3), (9, 0)),
    ((3, 2), (7, 1), (5, 1), (8, 1), (2, 3)),
    ((1, 3), (4, 2), (S1, 4), (0, 4)),
    ((6, 2), (3, 3), (10, 0), (2, 4), (7, 2)),
    ((5, 2), (12, 0), (S2, 0), (9, 1)),
    ((4, 3), (6, 3), (8, 2), (11, 0), (S2, 1)),
    (
        (7, 3), (13, 0), (5, 3), (11, 1), (S2, 2), (12, 1), (10, 1), (8, 3), (12, 2), (11, 2), (9, 2), (13, 1),
        (S2, 3), (10, 2), (6, 4), (12, 3), (5, 4), (9, 3), (8, 4), (11, 3), (13, 2), (S2, 4), (10, 3), (12, 4),
        (9, 4), (13, 3), (1, 5), (0, 5), (3, 5), (2, 5), (4, 5), (7, 5), (6, 5), (5, 5), (8, 5), (11, 5),
        (10, 5), (12, 5), (9, 5), (13, 5),
    ),
)

QB, VB, OB, AG, AS, XB, FG, FS, IB = range(9)
GO, GA, HX, HC, HF, HO, GP, GI, AT, AO = 0, 1, 2, 4, 6, 8, 10, 12, 14, 18
EXCHANGES = 19


def nn(left, right):
    return jnp.dot(left, right, preferred_element_type=F32)


def nt(left, right):
    return lax.dot_general(left, right, (((1,), (1,)), ((), ())), preferred_element_type=F32)


def tn(left, right):
    return lax.dot_general(left, right, (((0,), (0,)), ((), ())), preferred_element_type=F32)


def fold8(values):
    rows, width = values.shape
    return jnp.sum(values.reshape(rows // 8, 8, width), axis=0)


def halves_rows(order, k):
    return X in order[: k + 1] and order.index(X) < 3


def recv_shape(flow, k, rows):
    part, f, nf, start, cols, order = flow
    free = [2 for ax in BITS if ax not in order[: k + 1]]
    return (nf, *free, rows // 2 if halves_rows(order, k) else rows, cols)


def layer_kernel(groups, names, *refs):
    r = SimpleNamespace(**dict(zip(names, refs)))
    seq = lax.axis_index("seq")
    blk = lax.axis_index("blk")
    x = lax.div(blk, 2)
    c = lax.rem(blk, 2)
    hi = lax.div(seq, groups)
    own = {X: x, Y: lax.rem(hi, 2), Z0: lax.rem(lax.div(hi, 2), 2), Z1: lax.div(hi, 4)}
    peers = {
        C: (seq, blk + 1 - 2 * c),
        X: (seq, blk + 2 - 4 * x),
        Y: (seq + (1 - 2 * own[Y]) * groups, blk),
        Z0: (seq + (1 - 2 * own[Z0]) * 2 * groups, blk),
        Z1: (seq + (1 - 2 * own[Z1]) * 4 * groups, blk),
    }
    part_tok, width = r.xall.shape[2:]
    tok = 2 * part_tok
    groups_q = r.xall.shape[0]
    seq_len = groups_q * tok
    half = width // 2
    ff = r.wi.shape[1]
    pairs = half // 128
    own_heads = pl.ds(pl.multiple_of(c * half, 128), half)
    other_heads = pl.ds(pl.multiple_of((1 - c) * half, 128), half)

    def vec(i, start=0, size=width):
        return r.vec[:, pl.ds(width * i + start, size)]

    def pair_lanes(p, base=0):
        return pl.ds(pl.multiple_of(base * width + c * half + p * 128, 128), 128)

    def remote(src, dst, send, recv, peer):
        return pltpu.make_async_remote_copy(
            src_ref=src, dst_ref=dst, send_sem=send, recv_sem=recv, device_id=peers[peer], device_id_type=MESH
        )

    barrier = pltpu.get_barrier_semaphore()
    for peer in peers.values():
        pl.semaphore_signal(barrier, inc=1, device_id=peer, device_id_type=MESH)

    lcount = itertools.count()

    def fetch(src, dst):
        return pltpu.make_async_copy(src, dst, r.lsem.at[next(lcount)])

    def half_block(ref, seq_at, i):
        return ref.at[seq_at, pl.ds(i * part_tok, part_tok)]

    first = [fetch(half_block(r.hid, x, i), r.xall.at[i, c]) for i in range(2)]
    for p in range(pairs):
        for i, w in enumerate((r.wq, r.wk, r.wv)):
            first.append(fetch(w.at[:, pair_lanes(p)], r.wcat.at[:, pl.ds((3 * p + i) * 128, 128)]))
    second = [
        fetch(r.go.at[x], r.gown.at[0]),
        fetch(r.wo_in, r.wo),
        fetch(r.wi_in, r.wi),
        fetch(r.wx_in, r.wx),
    ]
    for copy in first + second:
        copy.start()
    params = (r.qb, r.vb, r.ob, r.ag, r.sh, r.xb, r.fg, r.fs, r.ib)
    third = [fetch(ref, r.raw.at[pl.ds(width * i, ref.shape[0])]) for i, ref in enumerate(params)]
    third.append(fetch(r.dg, r.kept))
    for copy in third:
        copy.start()
    pl.semaphore_wait(barrier, len(peers))

    def ex(i):
        if i == GO:
            src, dst, peer = r.go.at[1 - x], r.gown.at[1], X
        elif i == GA:
            src = dst = r.ga.at[:, c]
            peer = C
        elif i < HC:
            src, dst, peer = half_block(r.hid, 1 - x, i - HX), r.xall.at[2 + i - HX, c], X
        elif i < HF:
            src, dst, peer = half_block(r.hid, x, i - HC), r.xall.at[i - HC, c], C
        elif i < HO:
            src = dst = r.xall.at[2 + i - HF, c]
            peer = C
        elif i < GP:
            src, dst, peer = r.ga.at[2 + i - HO, c], half_block(r.hout, x, i - HO), X
        elif i < GI:
            at = pl.ds(2 * (i - GP), 2)
            src, dst, peer = r.gffn.at[at], r.xall.at[at, 1 - c], C
        elif i < AT:
            src, dst, peer = r.inn.at[2 + i - GI], half_block(r.gin, x, i - GI), X
        elif i < AO:
            src = dst = r.att.at[i - AT, 1 - c, :, own_heads]
            peer = C
        else:
            src = dst = r.att.at[:, c, :, own_heads]
            peer = C
        return remote(src, dst, r.ex_s.at[i], r.ex_r.at[i], peer)

    for i in (HX, HX + 1, HC, HC + 1, GO):
        ex(i).start()
    for copy in third:
        copy.wait()
    r.vec[...] = r.raw[...].astype(F32).reshape(1, r.raw.shape[0])
    r.sg8[...] = jnp.zeros_like(r.sg8)
    kept = jnp.where(r.kept[x] == 2, 0.0, 1.0).astype(F32)

    lane_head = lax.broadcasted_iota(jnp.int32, (tok, 128), 1) // HD
    ones = jnp.ones((seq_len, 128), BF)
    for p in range(pairs):
        r.vp[p, :, pl.ds(128, 128)] = ones

    def project(j):
        out = nn(r.xall[j].reshape(tok, width), r.wcat[...])
        at = pl.ds(pl.multiple_of(j * tok, tok), tok)
        for p in range(pairs):
            lanes = pl.ds(p * 128, 128)
            base = 3 * p * 128
            r.q[at, lanes] = (out[:, base : base + 128] + r.vec[:, pair_lanes(p, QB)]).astype(BF)
            key = out[:, base + 128 : base + 256].astype(BF)
            r.k[at, lanes] = key
            r.kt[lanes, at] = key.T
            r.vp[p, at, pl.ds(0, 128)] = (out[:, base + 256 : base + 384] + r.vec[:, pair_lanes(p, VB)]).astype(BF)

    def attend(j, start, count, begin_here, end_here):
        rows = pl.ds(pl.multiple_of(j * tok, tok), tok)
        keys = pl.ds(start, count)
        for p in range(pairs):
            lanes = pl.ds(p * 128, 128)
            out_ref = r.work.at[rows, lanes]
            top_ref = r.work.at[rows, pl.ds(half + p * 128, 128)]
            sum_lanes = pl.ds(pl.multiple_of(j * 128, 128), 128)
            sum_ref = (r.dva.at[rows], r.dka.at[rows], r.work.at[pl.ds(3 * tok, tok), sum_lanes])[p]
            qp = r.q[rows, lanes]
            tops, parts = [], []
            for h in range(2):
                qm = jnp.where(lane_head == h, qp, jnp.zeros_like(qp))
                s = nn(qm, r.kt[lanes, keys])
                top = jnp.max(s, axis=1, keepdims=True)
                pt = jnp.exp2((s - top) * SCALE2).astype(BF)
                tops.append(top)
                parts.append(nn(pt, r.vp[p, keys, :]))
            top = jnp.where(lane_head == 0, tops[0], tops[1])
            out = jnp.where(lane_head == 0, parts[0][:, :128], parts[1][:, :128])
            total = jnp.where(lane_head == 0, parts[0][:, 128:], parts[1][:, 128:])
            if not begin_here:
                old = top_ref[...]
                both = jnp.maximum(old, top)
                grow, shrink = jnp.exp2((top - both) * SCALE2), jnp.exp2((old - both) * SCALE2)
                out = out * grow + out_ref[...] * shrink
                total = total * grow + sum_ref[...] * shrink
                top = both
            if end_here:
                r.att[j, :, :, pair_lanes(p)] = (out / total).astype(BF).reshape(2, part_tok, 128)
                both = (top * SCALE2 + jnp.log2(total)).T
                for h in range(2):
                    r.lse[2 * p + h, :, rows] = both[h * HD : h * HD + 1]
            else:
                out_ref[...] = out
                top_ref[...] = top
                sum_ref[...] = total

    for copy in first:
        copy.wait()
    for i in range(2):
        ex(HC + i).wait_recv()

    @pl.loop(0, 2)
    def _(j):
        project(j)

    @pl.loop(0, 2)
    def _(j):
        attend(j, 0, 2 * tok, True, False)

    ex(HX).wait_recv()
    ex(HF).start()
    ex(HF).wait_recv()
    project(2)

    attend(2, 0, 3 * tok, True, False)
    ex(HX + 1).wait_recv()
    ex(HF + 1).start()
    ex(HF + 1).wait_recv()
    project(3)
    attend(3, 0, 4 * tok, True, True)
    ex(AT + 3).start()
    for j, start in ((2, 3 * tok), (1, 2 * tok), (0, 2 * tok)):
        attend(j, start, 4 * tok - start, False, True)
        ex(AT + j).start()
    ex(AO).start()

    for copy in second:
        copy.wait()

    def own_rows(i):
        return i // 2, pl.ds((i % 2) * part_tok, part_tok), pl.ds(i * part_tok, part_tok)

    def fold_in(i, values):
        at = pl.ds(width * i, values.shape[1])
        r.sg8[:, at] += fold8(values)

    def heads_out(heads):
        return nn(r.att[:, c, :, heads].reshape(2 * tok, half), r.wo[heads, :])

    acc, xh_ref = r.work.at[pl.ds(0, 2 * tok)], r.work.at[pl.ds(2 * tok, 2 * tok)]
    acc[...] = heads_out(own_heads)
    for j in range(groups_q):
        ex(AT + j).wait_recv()
    acc[...] += heads_out(other_heads)

    for i in range(4):
        which, inner, rows = own_rows(i)
        v = acc[rows, :] + vec(OB) + r.xall[i, c].astype(F32)
        cen = v - jnp.mean(v, axis=-1, keepdims=True)
        rstd = lax.rsqrt(jnp.mean(cen * cen, axis=-1, keepdims=True) + EPS)
        xh = cen * rstd
        normed = xh * vec(AG) + vec(AS)
        xh_ref[rows, :] = xh
        r.dva[rows, pl.ds(0, 1)] = rstd
        acc[rows, :] = normed
        r.inn[i] = normed.astype(BF)

    tile = 512

    def activate(j):
        start = pl.multiple_of(j * tile, tile)
        at = pl.ds(start, tile)
        pre = nn(r.inn[...].reshape(2 * tok, width), r.wi[:, at]) + r.vec[:, pl.ds(pl.multiple_of(width * IB + start, 128), tile)]
        phi = 0.5 + 0.5 * lax.erf(pre * math.sqrt(0.5))
        dens = jnp.exp2(pre * pre * (-0.5 * LOG2E)) * (1.0 / math.sqrt(2.0 * math.pi))
        r.act[:, at] = (pre * phi).astype(BF)
        r.gp[:, at] = (phi + pre * dens).astype(BF)

    @pl.loop(0, 2)
    def _(i):
        for j in range(ff // tile // 2):
            activate(i * (ff // tile // 2) + j)

    @pl.loop(0, width // 256)
    def _(j):
        at = pl.ds(pl.multiple_of(j * 256, 256), 256)
        acc[:, at] += nn(r.act[...], r.wx[:, at])

    ex(GO).wait_recv()
    for i in range(4):
        which, inner, rows = own_rows(i)
        xf = r.xall[i, c].astype(F32)
        v = acc[rows, :] + vec(XB)
        cen = v - jnp.mean(v, axis=-1, keepdims=True)
        rstd = lax.rsqrt(jnp.mean(cen * cen, axis=-1, keepdims=True) + EPS)
        xh = cen * rstd
        out = kept * (xh * vec(FG) + vec(FS)) + (1.0 - kept) * xf
        r.ga[i, c] = out.astype(BF)
        g = kept * r.gown[which, inner, :].astype(F32)
        fold_in(FG, g * xh)
        fold_in(FS, g)
        gx = g * vec(FG)
        m1 = jnp.mean(gx, axis=-1, keepdims=True)
        m2 = jnp.mean(gx * xh, axis=-1, keepdims=True)
        gs = rstd * (gx - m1 - xh * m2)
        low = gs.astype(BF)
        acc[rows, :] = gs
        r.gffn[i] = low
        fold_in(XB, low.astype(F32))

    ex(HO).start()
    ex(HO + 1).start()
    hout_local = [fetch(r.ga.at[i, c], half_block(r.hout, x, i)) for i in range(2)]
    for copy in hout_local:
        copy.start()

    rows_f, cols_f = r.dc.shape[-2:]
    x_rows = pl.ds(pl.multiple_of(x * (rows_f // 2), 16), rows_f // 2)

    def pieces(flow):
        f, nf = flow[1:3]
        return r.d2.at[c, pl.ds(f, nf)] if f < 8 else r.dc.at[pl.ds(f - 8, nf)]

    def view(flow, k, send):
        part, f, nf, start, cols, order = flow
        idx = [slice(None)] * 3
        row = pl.ds(0, rows_f)
        for j, ax in enumerate(order[: k + 1]):
            want = 1 - own[ax] if (j == k and send) else own[ax]
            if ax != X:
                idx[BITS.index(ax)] = want
            elif j < 3:
                row = pl.ds(pl.multiple_of(want * (rows_f // 2), 16), rows_f // 2)
        return (slice(None), *idx, row, pl.ds(start, cols))

    def hop(i, k):
        flow = FLOWS[i]
        src = pieces(flow).at[view(flow, k, True)]
        return remote(src, r.land[i][k], r.rs_s.at[i, k], r.rs_r.at[i, k], flow[5][k])

    def add_in(i, k):
        flow = FLOWS[i]
        nf, order = flow[2], flow[5]
        idx = list(view(flow, k, False))
        ref = pieces(flow)
        free = [ax for ax in BITS if ax not in order[: k + 1]]
        for n in range(nf):
            idx[0] = n
            for combo in itertools.product((0, 1), repeat=len(free)):
                for ax, bit in zip(free, combo):
                    idx[1 + BITS.index(ax)] = bit
                at = tuple(idx)
                ref[at] = ref[at] + r.land[i][k][(n, *combo, slice(None), slice(None))]

    def spread(i, k):
        part, f, nf, start, cols, order = FLOWS[i]
        rows = x_rows if k == 4 else pl.ds(0, rows_f)
        ref = r.sums.at[pl.ds(f, nf), c, rows, pl.ds(start, cols)]
        return remote(ref, ref, r.rs_s.at[i, k], r.rs_r.at[i, k], X if k == 4 else C)

    def save(i):
        part, f, nf, start, cols, order = FLOWS[i]
        at = (pl.ds(f, nf), slice(None), slice(None), pl.ds(start, cols))
        return pltpu.make_async_copy(r.sums.at[at], r.fin.at[at], r.rs_s.at[i, 7])

    def core_sum(i):
        part, f, nf, start, cols, order = FLOWS[i]
        at = pl.ds(f, nf)
        return remote(r.d2.at[1 - c, at], r.rc.at[at], r.rs_s.at[i, 6], r.rs_r.at[i, 6], C)

    def small(which, k):
        send, recv = (r.s1s, r.s1r) if which == S1 else (r.s2s, r.s2r)
        at = k if which == S1 else 5 + k
        return remote(send.at[k], recv.at[k], r.sm_s.at[at], r.sm_r.at[at], SMALL_ORDER[which][k])

    def step(i, k):
        if i < 0:
            send, recv = (r.s1s, r.s1r) if i == S1 else (r.s2s, r.s2r)
            small(i, k).wait_recv()
            send[k + 1] = send[k] + recv[k]
            if k < 4:
                small(i, k + 1).start()
            return
        flow = FLOWS[i]
        part, f, nf, start, cols, order = flow
        if k == -1:
            core_sum(i).wait_recv()
            ref = pieces(flow)
            for combo in itertools.product(range(nf), (0, 1), (0, 1), (0, 1)):
                ref[combo] = ref[combo] + r.rc[(f + combo[0], *combo[1:])]
            hop(i, 0).start()
        elif k < 3:
            hop(i, k).wait_recv()
            add_in(i, k)
            hop(i, k + 1).start()
        elif k == 3:
            hop(i, 3).wait_recv()
            rows = pl.ds(0, rows_f) if order[3] == X else x_rows
            at = pl.ds(start, cols)
            for n in range(nf):
                mine_part = pieces(flow)[(n, own[Z1], own[Z0], own[Y], rows, at)]
                r.sums[f + n, c, rows, at] = mine_part + r.land[i][3][n]
            spread(i, 5 if order[3] == X else 4).start()
        elif k == 4:
            spread(i, 4).wait_recv()
            spread(i, 5).start()
        else:
            spread(i, 5).wait_recv()
            save(i).start()

    plan = iter(PLAN)

    def tick():
        for i, k in next(plan):
            step(i, k)

    def begin(part):
        for i, flow in enumerate(FLOWS):
            if flow[0] == part:
                (core_sum(i) if flow[1] < 8 else hop(i, 0)).start()

    outer_rows = ff // 8

    @pl.loop(0, 2)
    def _(i):
        for j in range(4):
            at = pl.ds(pl.multiple_of((4 * i + j) * outer_rows, 128), outer_rows)
            val = tn(r.act[:, at], r.gffn[...].reshape(2 * tok, width)).astype(BF)
            for f in range(4):
                for h in range(2):
                    part = val[f * rows_f : (f + 1) * rows_f, h * cols_f : (h + 1) * cols_f]
                    r.d2[h, f, i, j // 2, j % 2] = part

    begin(OUTER)
    tick()

    tile = ff // 4

    @pl.loop(0, 2)
    def _(i):
        for j in range(2):
            start = pl.multiple_of((2 * i + j) * tile, tile)
            at = pl.ds(start, tile)
            gpre = (nt(r.gffn[...].reshape(2 * tok, width), r.wx[at, :]) * r.gp[:, at].astype(F32)).astype(BF)
            r.gp[:, at] = gpre
            r.sg8[:, pl.ds(pl.multiple_of(width * IB + start, 128), tile)] = fold8(gpre.astype(F32))

    tick()


    @pl.loop(0, width // 256)
    def _(j):
        at = pl.ds(pl.multiple_of(j * 256, 256), 256)
        acc[:, at] += nt(r.gp[...], r.wi[at, :])

    tick()
    ex(HO).wait_send()
    ex(HO + 1).wait_send()
    for copy in hout_local:
        copy.wait()
    for i in range(4):
        which, inner, rows = own_rows(i)
        g = acc[rows, :]
        xh = xh_ref[rows, :]
        fold_in(AG, g * xh)
        fold_in(AS, g)
        gx = g * vec(AG)
        m1 = jnp.mean(gx, axis=-1, keepdims=True)
        m2 = jnp.mean(gx * xh, axis=-1, keepdims=True)
        gs = r.dva[rows, pl.ds(0, 1)] * (gx - m1 - xh * m2)
        low = gs.astype(BF)
        acc[rows, :] = gs
        r.ga[i, c] = low
        fold_in(OB, low.astype(F32))

    xt = r.wi.at[:, pl.ds(0, seq_len)]
    xt[...] = r.xall[...].reshape(seq_len, width).T
    for i in range(2):
        ex(HF + i).wait_send()
    ex(GA).start()
    late = 2 * width
    r.s1s[0] = jnp.sum(r.sg8[:, pl.ds(late, r.s1s.shape[2])], axis=0, keepdims=True)
    small(S1, 0).start()
    tick()

    @pl.loop(0, 2)
    def _(i):
        for h in range(2):
            at = pl.ds(pl.multiple_of((2 * h + i) * tile, tile), tile)
            val = tn(r.inn[...].reshape(2 * tok, width), r.gp[:, at]).astype(BF)
            for m in range(2):
                part = val[:, m * cols_f : (m + 1) * cols_f]
                r.d2[h, 4 + 2 * i + m] = part.reshape(2, 2, 2, rows_f, cols_f)
        for n in range(2):

            @pl.when(i == n)
            def _():
                for g, flow in enumerate(FLOWS):
                    if flow[0] == INNER and (flow[1] + flow[2] - 1) // 2 == 2 + n:
                        core_sum(g).start()
                tick()


    def dqkv(p):
        rows = pl.ds(pl.multiple_of(lax.div(p, 2) * seq_len, 1024), seq_len)
        return r.wx.at[rows, pl.ds(pl.multiple_of(lax.rem(p, 2) * 384, 128), 384)]

    do = r.wx.at[pl.ds(seq_len, seq_len), pl.ds(384, half)]

    def upstream(core):
        val = nt(r.ga[:, core].reshape(2 * tok, width), r.wo[own_heads, :]).astype(BF)
        for j in range(groups_q):
            at = pl.ds(pl.multiple_of(j * tok + core * part_tok, part_tok), part_tok)
            do[at, :] = val[j * part_tok : (j + 1) * part_tok]

    upstream(c)
    tick()
    ex(GA).wait_recv()
    upstream(1 - c)

    for p in range(pairs):
        at = r.att[:, :, :, pair_lanes(p)].reshape(seq_len, 128)
        prod = (at.astype(F32) * do[:, pl.ds(p * 128, 128)].astype(F32)).T
        for h in range(2):
            r.delta[2 * p + h] = jnp.sum(prod[h * HD : (h + 1) * HD], axis=0, keepdims=True)
    tick()

    ex(AO).wait_recv()
    att_all = r.att[...].reshape(seq_len, width)
    ga_cols = r.ga[:, :, :, own_heads].reshape(seq_len, half)
    r.dc[3] = tn(att_all, ga_cols).astype(BF).reshape(2, 2, 2, rows_f, cols_f)
    begin(OUTPUT)
    tick()

    steps = [[next(plan) for _ in range(groups_q // 2 + 1)] for _ in range(pairs)]

    def tick_at(p, j):
        for n in range(pairs):
            if steps[n][j]:

                @pl.when(p == n)
                def _():
                    for i, k in steps[n][j]:
                        step(i, k)

    def backward(p, t):
        lanes = pl.ds(pl.multiple_of(p * 128, 128), 128)
        rows = pl.ds(pl.multiple_of(t * tok, tok), tok)
        qp = r.q[rows, lanes]
        dp = do[rows, lanes]
        kp = r.k[:, lanes]
        vp = r.vp[p, :, pl.ds(0, 128)]
        zero = jnp.zeros_like(qp)
        dqs = []
        for h in range(2):
            qm = jnp.where(lane_head == h, qp, zero)
            dm = jnp.where(lane_head == h, dp, zero)
            pt = jnp.exp2(nt(kp, qm) * SCALE2 - r.lse[2 * p + h, :, rows])
            ds = (pt * (nt(vp, dm) - r.delta[2 * p + h, :, rows])).astype(BF)
            r.dva[...] += nn(pt.astype(BF), dm)
            r.dka[...] += nn(ds, qm)
            dqs.append(nn(r.kt[pl.ds(pl.multiple_of(p * 128 + h * HD, HD), HD), :], ds))
        both = (jnp.concatenate(dqs, axis=0) * 0.125).astype(BF)
        dqkv(p)[rows, pl.ds(0, 128)] = both.T

    @pl.loop(0, pairs)
    def _(p):
        r.dva[...] = jnp.zeros_like(r.dva)
        r.dka[...] = jnp.zeros_like(r.dka)

        for t in range(groups_q):
            backward(p, t)
            if t % 2:
                tick_at(p, t // 2)

        dqkv(p)[:, pl.ds(128, 128)] = (r.dka[...] * 0.125).astype(BF)
        dqkv(p)[:, pl.ds(256, 128)] = r.dva[...].astype(BF)
        r.dc[p] = nn(xt[...], dqkv(p)[...]).astype(BF).reshape(2, 2, 2, rows_f, cols_f)
        r.sg8[:, pair_lanes(p, QB)] = fold8(dqkv(p)[:, pl.ds(0, 128)].astype(F32))
        r.sg8[:, pair_lanes(p, VB)] = fold8(dqkv(p)[:, pl.ds(256, 128)].astype(F32))
        for n in range(pairs):

            @pl.when(p == n)
            def _():
                begin(PAIR + n)
                if n == pairs - 1:
                    r.s2s[0] = jnp.sum(r.sg8[:, pl.ds(0, late)], axis=0, keepdims=True)
                    small(S2, 0).start()

        tick_at(p, 2)

    def partial(core, j):
        rows = [pl.ds(pl.multiple_of(n * tok + core * part_tok, part_tok), part_tok) for n in (2 * j, 2 * j + 1)]
        left = jnp.concatenate([r.wx[at, pl.ds(0, 768)] for at in rows], axis=0)
        right = jnp.concatenate([dqkv(2)[at, :] for at in rows], axis=0)
        return nt(left, r.wcat[:, pl.ds(0, 768)]) + nt(right, r.wcat[:, pl.ds(768, 384)])

    for i in (1, 0):
        r.gffn[pl.ds(2 * i, 2)] = partial(1 - c, i).astype(BF).reshape(2, part_tok, width)
        ex(GP + i).start()
    tick()
    for i in (1, 0):
        acc[pl.ds(i * tok, tok), :] += partial(c, i)
    tick()
    for i in (1, 0):
        ex(GP + i).wait_recv()
        for j in (2 * i, 2 * i + 1):
            which, inner, rows = own_rows(j)
            total = acc[rows, :] + r.xall[j, c].astype(F32) + (1.0 - kept) * r.gown[which, inner, :].astype(F32)
            r.inn[j] = total.astype(BF)
            if i:
                ex(GI + j - 2).start()
    gin_local = [fetch(r.inn.at[i], half_block(r.gin, x, i)) for i in range(2)]
    for copy in gin_local:
        copy.start()
    tick()
    tick()
    r.sout[:, pl.ds(0, late)] = r.s2s[5]
    r.sout[:, pl.ds(late, r.s1s.shape[2])] = r.s1s[5]

    for i in (HO, HO + 1, GI, GI + 1):
        ex(i).wait_recv()
    for copy in gin_local:
        copy.wait()
    for i in range(EXCHANGES):
        if i not in (HF, HF + 1, HO, HO + 1):
            ex(i).wait_send()
    for k in range(5):
        small(S1, k).wait_send()
        small(S2, k).wait_send()
    for i, flow in enumerate(FLOWS):
        for k in range(4):
            hop(i, k).wait_send()
        if flow[5][3] != X:
            spread(i, 4).wait_send()
        spread(i, 5).wait_send()
        save(i).wait()
        if flow[1] < 8:
            core_sum(i).wait_send()


def finish_kernel(n_seq, names, *refs):
    r = SimpleNamespace(**dict(zip(names, refs)))
    pairs = ((r.hout_in, r.hout), (r.gin_in, r.gin))
    arrive = [pltpu.make_async_copy(pair[0], r.through.at[i], r.sem.at[i]) for i, pair in enumerate(pairs)]
    leave = [pltpu.make_async_copy(r.through.at[i], pair[1], r.sem.at[2 + i]) for i, pair in enumerate(pairs)]
    flat = pltpu.make_async_copy(r.sout, r.flat, r.sem.at[10 + PIECES])
    flat.start()
    for copy in arrive:
        copy.start()
    for before, after in zip(arrive, leave):
        before.wait()
        after.start()
    rows_f, cols_f = r.fin.shape[2:]
    half = cols_f
    outs = (r.outer, r.inner, r.output, r.query, r.key, r.value)
    made = (r.t_outer, r.t_inner, r.t_output, r.t_query, r.t_key, r.t_value)
    done = [pltpu.make_async_copy(src, dst, r.sem.at[4 + i]) for i, (src, dst) in enumerate(zip(made, outs))]

    def take(f):
        return pltpu.make_async_copy(r.fin.at[f], r.got.at[f], r.sem.at[10 + f])

    for f in range(PIECES):
        take(f).start()
    for f in range(4):
        take(f).wait()
        for h in range(2):
            r.t_outer[pl.ds(f * rows_f, rows_f), pl.ds(h * half, half)] = r.got[f, h].astype(F32)
    done[0].start()
    for f in range(4):
        take(4 + f).wait()
        for h in range(2):
            r.t_inner[:, pl.ds((4 * h + f) * cols_f, cols_f)] = r.got[4 + f, h].astype(F32)
    done[1].start()
    for f in range(8, PIECES):
        take(f).wait()
    for h in range(2):
        r.t_output[:, pl.ds(h * half, half)] = r.got[11, h].astype(F32)
    done[2].start()
    for i, ref in enumerate(made[3:]):
        for h in range(2):
            for p in range(half // 128):
                part = r.got[8 + p, h, :, pl.ds(i * 128, 128)].astype(F32)
                ref[:, pl.ds(h * half + p * 128, 128)] = part
        done[3 + i].start()
    seq = lax.axis_index("seq")
    width = 2 * half
    share = width // n_seq
    flat.wait()
    for i in range(8):
        r.rows[pl.ds(i, 1), :] = r.flat[:, pl.ds(i * width, width)]
    turned = pltpu.roll(r.rows[...], lax.rem(width - seq * share, width), 1)
    for i, ref in enumerate((r.t_qb, r.t_vb, r.t_ob, r.t_ag, r.t_sh, r.t_xb, r.t_fg, r.t_fs)):
        ref[...] = turned[i, :share]
    ib = r.ib.shape[0]
    full = r.flat.shape[1] - 8 * width
    r.wide[...] = jnp.broadcast_to(r.flat[:, pl.ds(8 * width, full)], (8, full))
    r.t_ib[...] = pltpu.roll(r.wide[...], lax.rem(full - seq * ib, full), 1)[0, :ib]
    vectors = (r.qb, r.vb, r.ob, r.ag, r.sh, r.xb, r.fg, r.fs, r.ib)
    shares = (r.t_qb, r.t_vb, r.t_ob, r.t_ag, r.t_sh, r.t_xb, r.t_fg, r.t_fs, r.t_ib)
    for i, (src, dst) in enumerate(zip(shares, vectors)):
        done.append(pltpu.make_async_copy(src, dst, r.sem.at[11 + PIECES + i]))
        done[-1].start()
    for copy in leave + done:
        copy.wait()


def call(kernel, ins, outs, scratch, params, name, land=()):
    names = [*ins, *outs, *scratch]

    def body(*refs):
        extra = refs[len(names) :]
        shelf = iter(extra)
        nested = [[next(shelf) for _ in group] for group in land]
        kernel([*names, *(("land",) if land else ())], *refs[: len(names)], *((nested,) if land else ()))

    res = pl.pallas_call(
        body,
        out_shape=[jax.ShapeDtypeStruct(e[0], e[1]) for e in outs.values()],
        in_specs=[e[1] for e in ins.values()],
        out_specs=[e[2] for e in outs.values()],
        scratch_shapes=[*scratch.values(), *(e for group in land for e in group)],
        compiler_params=params,
        name=name,
    )(*[e[0] for e in ins.values()])
    return SimpleNamespace(**dict(zip(outs, res)))


def build(mesh):
    n_seq = mesh.shape["seq"]
    groups = n_seq // 8

    def local(
        hidden_in,
        depth_group,
        query_weight,
        query_bias,
        key_weight,
        value_weight,
        value_bias,
        output_weight,
        output_bias,
        attn_gain,
        attn_shift,
        inner_weight,
        inner_bias,
        outer_weight,
        outer_bias,
        final_gain,
        final_shift,
        grad_out,
    ):
        seqs, tok, width = hidden_in.shape
        ff = inner_weight.shape[1]
        seq_len = 4 * tok
        half = width // 2
        heads = half // HD
        pairs = half // 128
        rows_f, cols_f = width // 8, half
        small, late = 8 * width + ff, 2 * width
        hbm = pl.BlockSpec(memory_space=pl.ANY)
        vmem = pl.BlockSpec(memory_space=pltpu.VMEM)
        v = pltpu.VMEM
        dma = pltpu.SemaphoreType.DMA
        o = call(
            lambda *refs: layer_kernel(groups, *refs),
            dict(
                qb=(query_bias, hbm),
                vb=(value_bias, hbm),
                ob=(output_bias, hbm),
                ag=(attn_gain, hbm),
                sh=(attn_shift, hbm),
                xb=(outer_bias, hbm),
                fg=(final_gain, hbm),
                fs=(final_shift, hbm),
                ib=(inner_bias, hbm),
                dg=(depth_group, hbm),
                hid=(hidden_in, hbm),
                go=(grad_out, hbm),
                wq=(query_weight, hbm),
                wk=(key_weight, hbm),
                wv=(value_weight, hbm),
                wo_in=(output_weight, hbm),
                wi_in=(inner_weight, hbm),
                wx_in=(outer_weight, hbm),
            ),
            dict(
                hout=((seqs, tok, width), BF, hbm),
                gin=((seqs, tok, width), BF, hbm),
                fin=((PIECES, 2, rows_f, cols_f), BF, hbm),
                sout=((1, small), F32, vmem),
            ),
            dict(
                kept=pltpu.SMEM((seqs,), jnp.int32),
                raw=v((small,), BF),
                vec=v((1, small), F32),
                xall=v((4, 2, tok // 2, width), BF),
                gown=v((2, tok, width), BF),
                wcat=v((width, 3 * half), BF),
                wo=v((width, width), BF),
                wi=v((width, ff), BF),
                wx=v((ff, width), BF),
                q=v((seq_len, half), BF),
                k=v((seq_len, half), BF),
                kt=v((half, seq_len), BF),
                vp=v((pairs, seq_len, 256), BF),
                lse=v((heads, 1, seq_len), F32),
                delta=v((heads, 1, seq_len), F32),
                att=v((4, 2, tok // 2, width), BF),
                ga=v((4, 2, tok // 2, width), BF),
                act=v((2 * tok, ff), BF),
                gp=v((2 * tok, ff), BF),
                inn=v((4, tok // 2, width), BF),
                gffn=v((4, tok // 2, width), BF),
                work=v((4 * tok, width), F32),
                dka=v((seq_len, 128), F32),
                dva=v((seq_len, 128), F32),
                d2=v((2, 8, 2, 2, 2, rows_f, cols_f), BF),
                rc=v((8, 2, 2, 2, rows_f, cols_f), BF),
                dc=v((4, 2, 2, 2, rows_f, cols_f), BF),
                sg8=v((8, small), F32),
                s1s=v((6, 1, small - late), F32),
                s1r=v((5, 1, small - late), F32),
                s2s=v((6, 1, late), F32),
                s2r=v((5, 1, late), F32),
                lsem=dma((20 + 3 * pairs,)),
                ex_s=dma((EXCHANGES,)),
                ex_r=dma((EXCHANGES,)),
                sums=v((PIECES, 2, rows_f, cols_f), BF),
                rs_s=dma((len(FLOWS), 8)),
                rs_r=dma((len(FLOWS), 7)),
                sm_s=dma((10,)),
                sm_r=dma((10,)),
            ),
            pltpu.CompilerParams(collective_id=0, has_side_effects=True, vmem_limit_bytes=64 * 1024 * 1024),
            "layer",
            [[v(recv_shape(flow, k, rows_f), BF) for k in range(4)] for flow in FLOWS],
        )

        rows = [[g * groups + i for i in range(groups)] for g in range(8)]
        sout = o.sout
        if groups > 1:
            sout = lax.psum(sout, "seq", axis_index_groups=rows)
        mat, one = ((rows_f, width), F32, hbm), ((width // n_seq,), F32, hbm)
        staged, short = v((rows_f, width), F32), v((width // n_seq,), F32)
        f = call(
            lambda *refs: finish_kernel(n_seq, *refs),
            dict(hout_in=(o.hout, hbm), gin_in=(o.gin, hbm), fin=(o.fin, hbm), sout=(sout, hbm)),
            dict(
                hout=(o.hout.shape, BF, hbm),
                gin=(o.gin.shape, BF, hbm),
                query=mat,
                key=mat,
                value=mat,
                output=mat,
                inner=((rows_f, ff), F32, hbm),
                outer=((ff // 8, width), F32, hbm),
                qb=one,
                vb=one,
                ob=one,
                ag=one,
                sh=one,
                xb=one,
                fg=one,
                fs=one,
                ib=((ff // n_seq,), F32, hbm),
            ),
            dict(
                sem=dma((20 + PIECES,)),
                flat=v((1, small), F32),
                t_qb=short,
                t_vb=short,
                t_ob=short,
                t_ag=short,
                t_sh=short,
                t_xb=short,
                t_fg=short,
                t_fs=short,
                t_ib=v((ff // n_seq,), F32),
                got=v((PIECES, 2, rows_f, cols_f), BF),
                t_query=staged,
                t_key=staged,
                t_value=staged,
                t_output=staged,
                t_inner=v((rows_f, ff), F32),
                t_outer=v((ff // 8, width), F32),
                through=v((2, seqs, tok, width), BF),
                rows=v((8, width), F32),
                wide=v((8, ff), F32),
            ),
            pltpu.CompilerParams(vmem_limit_bytes=64 * 1024 * 1024),
            "finish",
        )

        def across(values):
            if groups == 1:
                return values
            return lax.psum_scatter(values, "seq", scatter_dimension=0, axis_index_groups=rows, tiled=True)

        return (
            f.hout,
            f.gin,
            across(f.query),
            f.qb,
            across(f.key),
            across(f.value),
            f.vb,
            across(f.output),
            f.ob,
            f.ag,
            f.sh,
            across(f.inner),
            f.ib,
            across(f.outer),
            f.xb,
            f.fg,
            f.fs,
        )

    return local


def solution(mesh):
    rows = P("seq", "blk", None)
    placed = (rows, P("seq"), *([P()] * 15), rows)
    mat, one = P("seq", None), P("seq")
    return jax.shard_map(
        build(mesh),
        mesh=mesh,
        in_specs=placed,
        out_specs=(rows, rows, mat, one, mat, mat, one, mat, one, one, one, mat, one, mat, one, one, one),
        check_vma=False,
    )
```

time: 120 us -> 118 us (0.983)
  Pallas kernels: 119 us -> 117 us
    pallas_call x2, Pallas kernels: 119 us -> 117 us  [call(): pl.pallas_call(body, out_shape=[jax.ShapeDtypeStruct(e[0], e[1]) for e in...]
where the time goes in v1:
time: 118 us
  Pallas kernels  117 us (99%)
    pallas_call x2, Pallas kernels, call(): pl.pallas_call(body, out_shape=[jax.ShapeDtypeStruct(e[0], e[1]) for e in...  117 us

profile of v1, /device:TPU:1, one launch (start us, length us, event | category | flops | bytes accessed | tf_op | source)
XLA Modules:
  0.0 118.2 jit_solution(9136628787589328747)
XLA Ops:
  0.7 112.4 %layer.1 = (bf16[2,256,768]{2,1,0:T(8,128)(2,1)}, bf16[2,256,768]{2,1,0:T(8,128)(2,1)}, bf16[12,2,96,384]{3,2,1,0:T(8,128)(2,1)}, f32[1,9216]{1,0:T(1,128)}) custom-call(bf16[768]{0:T(1024)(128)(2,1)} %refs_0_.1, bf16[768]{0:T(1024)(128)(2,1)} %refs_1_.1, bf16[768]{0:T(1024)(128)(2,1)} %refs_2_.1, bf16[768]{0:T(1024)(128)(2,1)} %refs_3_.1, ...), custom_call_target="tpu_custom_call" | custom-call | tf_op jit(solution)/shard_map/layer/pallas_call | solution.py:773
  113.1 5.0 %finish.1 = (bf16[2,256,768]{2,1,0:T(8,128)(2,1)}, bf16[2,256,768]{2,1,0:T(8,128)(2,1)}, f32[96,768]{1,0:T(8,128)}, f32[96,768]{1,0:T(8,128)}, f32[96,768]{1,0:T...) custom-call(bf16[2,256,768]{2,1,0:T(8,128)(2,1)} %get-tuple-element., ...), custom_call_target="tpu_custom_call" | custom-call | tf_op jit(solution)/shard_map/finish/pallas_call | solution.py:773

commit v2 on v1

--- a/solution.py
+++ b/solution.py
@@ -25,19 +25,19 @@
 S1, S2 = -1, -2
 SMALL_ORDER = {S1: (C, Y, Z0, Z1, X), S2: (X, C, Y, Z0, Z1)}
 FLOWS = (
-    (OUTER, 0, 1, 0, 384, (Z0, X, Z1, Y)),
-    (OUTER, 1, 1, 0, 384, (Y, Z1, Z0, X)),
-    (OUTER, 2, 1, 0, 384, (X, Y, Z0, Z1)),
+    (OUTER, 0, 1, 0, 384, (Y, X, Z1, Z0)),
+    (OUTER, 1, 1, 0, 384, (Z0, Z1, Y, X)),
+    (OUTER, 2, 1, 0, 384, (X, Z0, Z1, Y)),
     (OUTER, 3, 1, 0, 384, (Z0, Y, Z1, X)),
-    (INNER, 4, 1, 0, 384, (Y, Z1, Z0, X)),
-    (INNER, 5, 1, 0, 384, (Y, X, Z0, Z1)),
-    (INNER, 6, 1, 0, 384, (X, Y, Z0, Z1)),
-    (INNER, 7, 1, 0, 384, (Z0, Y, Z1, X)),
-    (OUTPUT, 11, 1, 0, 384, (X, Z0, Y, Z1)),
-    (PAIR, 8, 1, 0, 384, (X, Y, Z0, Z1)),
-    (PAIR + 1, 9, 1, 0, 384, (Y, Z0, Z1, X)),
-    (PAIR + 2, 10, 1, 0, 128, (Z0, Y, Z1, X)),
-    (PAIR + 2, 10, 1, 128, 128, (X, Z1, Y, Z0)),
+    (INNER, 4, 1, 0, 384, (Y, Z0, Z1, X)),
+    (INNER, 5, 1, 0, 384, (X, Y, Z1, Z0)),
+    (INNER, 6, 1, 0, 384, (X, Y, Z1, Z0)),
+    (INNER, 7, 1, 0, 384, (X, Z0, Y, Z1)),
+    (OUTPUT, 11, 1, 0, 384, (Y, Z0, X, Z1)),
+    (PAIR, 8, 1, 0, 384, (Y, X, Z1, Z0)),
+    (PAIR + 1, 9, 1, 0, 384, (Z0, Y, Z1, X)),
+    (PAIR + 2, 10, 1, 0, 128, (Y, Z0, Z1, X)),
+    (PAIR + 2, 10, 1, 128, 128, (X, Y, Z1, Z0)),
     (PAIR + 2, 10, 1, 256, 128, (Y, Z0, Z1, X)),
 )
 PLAN = (
@@ -53,20 +53,20 @@
     ((2, 0),),
     ((0, 1), (1, 1), (4, 0), (3, 0), (S1, 2)),
     (),
-    ((6, 0), (5, 0), (0, 2)),
-    ((2, 1), (7, 0)),
-    ((8, 0), (3, 1), (1, 2), (4, 1)),
-    ((S1, 3), (6, 1), (2, 2), (0, 3), (9, 0)),
-    ((3, 2), (7, 1), (5, 1), (8, 1), (2, 3)),
-    ((1, 3), (4, 2), (S1, 4), (0, 4)),
-    ((6, 2), (3, 3), (10, 0), (2, 4), (7, 2)),
-    ((5, 2), (12, 0), (S2, 0), (9, 1)),
-    ((4, 3), (6, 3), (8, 2), (11, 0), (S2, 1)),
+    ((2, 1), (5, 0), (8, 0), (0, 2), (1, 2)),
+    ((S1, 3), (4, 1), (3, 1), (6, 0)),
+    ((2, 2),),
+    ((8, 1), (0, 3), (4, 2), (9, 0), (7, 0)),
+    ((1, 3), (S1, 4), (3, 2), (5, 1), (8, 2)),
+    ((0, 4), (6, 1), (4, 3), (2, 3)),
+    ((10, 0),),
+    ((9, 1), (5, 2), (11, 0), (3, 3), (8, 3)),
+    ((13, 0),),
     (
-        (7, 3), (13, 0), (5, 3), (11, 1), (S2, 2), (12, 1), (10, 1), (8, 3), (12, 2), (11, 2), (9, 2), (13, 1),
-        (S2, 3), (10, 2), (6, 4), (12, 3), (5, 4), (9, 3), (8, 4), (11, 3), (13, 2), (S2, 4), (10, 3), (12, 4),
-        (9, 4), (13, 3), (1, 5), (0, 5), (3, 5), (2, 5), (4, 5), (7, 5), (6, 5), (5, 5), (8, 5), (11, 5),
-        (10, 5), (12, 5), (9, 5), (13, 5),
+        (12, 0), (S2, 0), (7, 1), (2, 4), (S2, 1), (6, 2), (8, 4), (10, 1), (5, 3), (12, 1), (11, 1), (9, 2),
+        (7, 2), (S2, 2), (13, 1), (10, 2), (6, 3), (12, 2), (9, 3), (11, 2), (S2, 3), (5, 4), (7, 3), (12, 3),
+        (13, 2), (10, 3), (S2, 4), (6, 4), (9, 4), (11, 3), (7, 4), (12, 4), (13, 3), (1, 5), (0, 5), (4, 5),
+        (3, 5), (2, 5), (8, 5), (5, 5), (10, 5), (6, 5), (9, 5), (11, 5), (7, 5), (12, 5), (13, 5),
     ),
 )
 

time: 118 us -> 118 us (level)
  no operation moved by 1% of the time
where the time goes in v2:
time: 118 us; the launch traced here: 117 us
  Pallas kernels  117 us (99%)
    pallas_call x2, Pallas kernels, call(): pl.pallas_call(body, out_shape=[jax.ShapeDtypeStruct(e[0], e[1]) for e in...  117 us

profile of v2, /device:TPU:1, one launch (start us, length us, event | category | flops | bytes accessed | tf_op | source)
XLA Modules:
  0.0 117.5 jit_solution(12480812340141017384)
XLA Ops:
  0.7 111.6 %layer.1 = (bf16[2,256,768]{2,1,0:T(8,128)(2,1)}, bf16[2,256,768]{2,1,0:T(8,128)(2,1)}, bf16[12,2,96,384]{3,2,1,0:T(8,128)(2,1)}, f32[1,9216]{1,0:T(1,128)}) custom-call(bf16[768]{0:T(1024)(128)(2,1)} %refs_0_.1, bf16[768]{0:T(1024)(128)(2,1)} %refs_1_.1, bf16[768]{0:T(1024)(128)(2,1)} %refs_2_.1, bf16[768]{0:T(1024)(128)(2,1)} %refs_3_.1, ...), custom_call_target="tpu_custom_call" | custom-call | tf_op jit(solution)/shard_map/layer/pallas_call | solution.py:773
  112.3 5.0 %finish.1 = (bf16[2,256,768]{2,1,0:T(8,128)(2,1)}, bf16[2,256,768]{2,1,0:T(8,128)(2,1)}, f32[96,768]{1,0:T(8,128)}, f32[96,768]{1,0:T(8,128)}, f32[96,768]{1,0:T...) custom-call(bf16[2,256,768]{2,1,0:T(8,128)(2,1)} %get-tuple-element., ...), custom_call_target="tpu_custom_call" | custom-call | tf_op jit(solution)/shard_map/finish/pallas_call | solution.py:773
